TPU v7x, 32 devices: a whole 2x2x4 slice. The times are simulated.
32 devices in a mesh: pair: 2 (over y), src: 8 (over z, x), tgt: 2 (over core).
Axes of the slice: x: 2, y: 2, z: 4, core: 2. Of those that a mesh axis runs over, the one named last changes fastest.
Arguments:
- source_features: bfloat16 [64, 8, 256], P('pair', 'src'), parts along dimension 0, may hold values from -6 to 6
- target_features: bfloat16 [128, 8, 256], P(('pair', 'tgt'), 'src'), parts along dimension 0, may hold values from -6 to 6
- source_rows: int32 [8], P('pair'), parts along dimension 0, may hold values from 0 to 31
- target_cols: int32 [16], P('pair'), parts along dimension 0, may hold values from 0 to 7, each once
- target_kernel_one: bfloat16 [3, 3, 16, 16], replicated, may hold values from -0.75 to 0.75
- source_kernel: bfloat16 [3, 3, 16, 16], replicated, may hold values from -0.75 to 0.75
- target_kernel_two: bfloat16 [3, 3, 16, 16], replicated, may hold values from -0.75 to 0.75
Outputs:
- filtered: bfloat16 [8, 8, 64, 128], P('pair', 'src', 'tgt'), parts along dimension 0
There are 2 independent parts, one for each index of `pair`. A program takes and returns all parts, laid end to end along the dimension named above; an argument that names none is the same for every part. Nothing has to cross between parts.
Inputs may be any that keep to these rules, and one draw needn't show every extreme that they name: `target_cols`: each column index appears once.
All inputs are finite; a program needn't handle non-finite values.
Results may differ from a plain program's by a relative error of at most 0.0074.
Values may be sent and summed in bfloat16 or wider, within the bound.
A program may use at most 128 MiB of HBM per device.

v0:
```python
import functools

import jax
import jax.numpy as jnp
from jax import lax
from jax.experimental import pallas as pl
from jax.experimental.pallas import tpu as pltpu
from jax.sharding import PartitionSpec as P

MESH = pl.DeviceIdType.MESH
LANES = 128
HALO = 16
BF16 = jnp.bfloat16
F32 = jnp.float32


def iota(shape, dim):
    return lax.broadcasted_iota(jnp.int32, shape, dim)


def dot(a, b):
    return jnp.dot(a, b, preferred_element_type=F32)


def kernel(
    src_count,
    tgt_count,
    breadth,
    window_rows,
    groups,
    rows_hbm,
    cols_hbm,
    tgt_hbm,
    src_hbm,
    k1_hbm,
    ks_hbm,
    k2_hbm,
    out_ref,
    rows_ref,
    cols_ref,
    buf,
    sbuf,
    taps,
    vol,
    sec,
    stage,
    w1,
    w2,
    w3,
    local_sem,
    send_sem,
    recv_sem,
    halo_send,
    halo_recv,
    src_send,
    src_recv,
):
    rows, features = tgt_hbm.shape
    map_rows = src_hbm.shape[0]
    channels = features // groups
    span = rows + HALO
    width = vol.shape[1]
    column_lanes = window_rows * groups
    per_block = LANES // groups
    chunks = breadth // per_block
    chunk_rows = per_block * span
    me = lax.axis_index("src")
    half = lax.axis_index("tgt")
    main = pl.ds(pl.multiple_of(half * HALO, HALO), rows)

    def peer(d):
        return lax.rem(me + d, src_count)

    barrier = pltpu.get_barrier_semaphore()
    for d in range(1, src_count):
        pl.semaphore_signal(barrier, inc=1, device_id={"src": peer(d)}, device_id_type=MESH)
    if tgt_count > 1:
        pl.semaphore_signal(barrier, inc=1, device_id={"tgt": 1 - half}, device_id_type=MESH)

    own = [
        pltpu.make_async_copy(tgt_hbm, buf.at[me, main], local_sem.at[0]),
        pltpu.make_async_copy(src_hbm, sbuf.at[1], local_sem.at[1]),
        pltpu.make_async_copy(k1_hbm, taps.at[0], local_sem.at[2]),
        pltpu.make_async_copy(ks_hbm, taps.at[1], local_sem.at[3]),
        pltpu.make_async_copy(k2_hbm, taps.at[2], local_sem.at[4]),
        pltpu.make_async_copy(rows_hbm, rows_ref, local_sem.at[5]),
        pltpu.make_async_copy(cols_hbm, cols_ref, local_sem.at[6]),
    ]
    for copy in own:
        copy.start()
    pl.semaphore_wait(barrier, src_count - 1 + (1 if tgt_count > 1 else 0))

    edge = pl.ds(pl.multiple_of(half * HALO + (1 - half) * (rows - HALO), HALO), HALO)
    landing = pl.ds(pl.multiple_of(half * rows, HALO), HALO)

    to_right = pltpu.make_async_remote_copy(
        src_ref=src_hbm, dst_ref=sbuf.at[0], send_sem=src_send.at[0], recv_sem=src_recv.at[0],
        device_id={"src": lax.rem(me + 1, src_count)}, device_id_type=MESH,
    )
    to_left = pltpu.make_async_remote_copy(
        src_ref=src_hbm, dst_ref=sbuf.at[2], send_sem=src_send.at[1], recv_sem=src_recv.at[1],
        device_id={"src": lax.rem(me + src_count - 1, src_count)}, device_id_type=MESH,
    )
    sends = []
    for d in range(1, src_count):
        sends.append(
            pltpu.make_async_remote_copy(
                src_ref=tgt_hbm, dst_ref=buf.at[me, main], send_sem=send_sem.at[d],
                recv_sem=recv_sem.at[d], device_id={"src": peer(d)}, device_id_type=MESH,
            )
        )
    order = sorted(range(1, src_count), key=lambda d: -min(d, src_count - d))
    to_right.start()
    to_left.start()
    for d in order:
        sends[d - 1].start()

    def forward(d, source):
        column = lax.rem(me + src_count - d, src_count)
        return pltpu.make_async_remote_copy(
            src_ref=source(column), dst_ref=buf.at[column, landing], send_sem=halo_send.at[d],
            recv_sem=halo_recv.at[d], device_id={"tgt": 1 - half}, device_id_type=MESH,
        )

    forwards = []
    if tgt_count > 1:
        offset = pl.multiple_of((1 - half) * (rows - HALO), HALO)
        forwards.append(forward(0, lambda column: tgt_hbm.at[pl.ds(offset, HALO)]))
        forwards[0].start()

    zero_block = jnp.zeros((span, width), BF16)
    for ref in (vol, sec):
        ref[pl.ds(0, span), :] = zero_block
        ref[pl.ds((breadth + 1) * span, span), :] = zero_block
    for copy in own[2:5]:
        copy.wait()
    expand = (iota((groups, width), 1) % groups == iota((groups, width), 0)).astype(BF16)
    spread = [dot(taps[i], expand).astype(BF16) for i in range(3)]
    lane_group = iota((groups, width), 1) // groups
    nothing = jnp.zeros((groups, width), BF16)

    def tap(i, a, b):
        start = (a * 3 + b) * groups
        return spread[i][start : start + groups]

    for a in range(3):
        for b in range(3):
            for j in range(width // groups):
                w1[a, pl.ds(b * width + j * groups, groups), :] = jnp.where(
                    lane_group == j, tap(0, a, b), nothing
                )
    for j in range(width // groups):
        k, h = divmod(j, window_rows)
        two = nothing
        three = [nothing[:, :LANES]] * 3
        if k < 3:
            for a in range(3):
                two = jnp.where(lane_group % window_rows == h - a + 1, tap(1, a, k), two)
                three[a] = jnp.where(
                    (lane_group % window_rows == h)[:, :LANES], tap(2, a, k)[:, :LANES], three[a]
                )
        w2[pl.ds(j * groups, groups), :] = two
        for a in range(3):
            w3[pl.ds(j * groups, groups), pl.ds(a * LANES, LANES)] = three[a]

    def valid(extra):
        position = iota((chunk_rows, width), 0) % span
        low = half * (HALO - extra)
        return (position >= low) & (position < low + rows + extra)

    own[1].wait()
    own[5].wait()
    own[6].wait()
    to_right.wait()
    to_left.wait()
    row_of = iota((column_lanes, map_rows), 0) // groups
    wanted = jnp.zeros((column_lanes, map_rows), jnp.int32)
    for h in range(window_rows):
        wanted = jnp.where(row_of == h, rows_ref[h], wanted)
    select = (iota((column_lanes, map_rows), 1) == wanted).astype(BF16)
    same_group = (
        iota((column_lanes, features), 1) // channels == iota((column_lanes, features), 0) % groups
    )
    parts = []
    for k in range(3):
        keep = same_group
        if k == 0:
            keep = keep & (me > 0)
        if k == 2:
            keep = keep & (me < src_count - 1)
        parts.append(jnp.where(keep, dot(select, sbuf[k]), 0.0).astype(BF16))
    if width > 3 * column_lanes:
        parts.append(jnp.zeros((width - 3 * column_lanes, features), BF16))
    weights = jnp.concatenate(parts, axis=0)

    own[0].wait()
    for d in range(1, src_count):
        sends[d - 1].wait_recv()
        if tgt_count > 1:
            copy = forward(d, lambda column: buf.at[column, edge])
            copy.start()
            forwards.append(copy)
    for copy in forwards:
        copy.wait_recv()

    def volume_chunk(chunk):
        window = jnp.concatenate(
            [buf[cols_ref[chunk * per_block + i]] for i in range(per_block)], axis=0
        )
        scores = lax.dot_general(
            window, weights, (((1,), (1,)), ((), ())), preferred_element_type=F32
        ) * (channels ** -0.5)
        vol[pl.ds(pl.multiple_of((chunk * per_block + 1) * span, span), chunk_rows), :] = (
            jnp.where(valid(2), scores, 0.0).astype(BF16)
        )

    def at(chunk, b):
        return pl.ds(pl.multiple_of((chunk * per_block + b) * span, span), chunk_rows)

    def shifted(parts):
        total = parts[1] + pltpu.roll(parts[0], 1, 0)
        return total + pltpu.roll(parts[2], chunk_rows - 1, 0)

    def middle_chunk(chunk):
        window = jnp.concatenate([vol[at(chunk, b), :] for b in range(3)], axis=1)
        one = shifted([dot(window, w1[a]) for a in range(3)])
        one = jnp.maximum(one, 0.0).astype(BF16)
        two = jnp.maximum(dot(one, w2[...]), 0.0)
        sec[at(chunk, 1), :] = jnp.where(valid(1), two, 0.0).astype(BF16)

    def last_chunk(chunk):
        which = iota((chunk_rows, width), 1) // column_lanes
        window = jnp.where(
            which == 0,
            sec[at(chunk, 0), :],
            jnp.where(which == 1, sec[at(chunk, 1), :], sec[at(chunk, 2), :]),
        )
        three = dot(window, w3[...])
        three = shifted([three[:, a * LANES : (a + 1) * LANES] for a in range(3)])
        stage[...] = jnp.maximum(three, 0.0)
        pieces = [
            stage[pl.ds(pl.multiple_of(i * span + half * HALO, HALO), rows), :]
            for i in range(per_block)
        ]
        group = iota((rows, LANES), 1) // groups
        rolled = []
        for d in range(window_rows):
            mixed = pieces[d % per_block]
            for j in range(1, per_block):
                mixed = jnp.where(group == j, pieces[(j + d) % per_block], mixed)
            rolled.append(pltpu.roll(mixed, d * groups, 1) if d else mixed)
        for h in range(window_rows):
            total = rolled[0]
            for d in range(1, window_rows):
                total = jnp.where((group - h) % window_rows == d, rolled[d], total)
            out_ref[h, :, pl.ds(pl.multiple_of(chunk * LANES, LANES), LANES)] = total.astype(BF16)

    for step in (volume_chunk, middle_chunk, last_chunk):
        if chunks == 1:
            step(0)
        else:
            pl.loop(0, chunks)(step)

    for copy in sends:
        copy.wait_send()
    for copy in forwards:
        copy.wait_send()


def local(
    src_count,
    tgt_count,
    source_features,
    target_features,
    source_rows,
    target_cols,
    target_kernel_one,
    source_kernel,
    target_kernel_two,
):
    groups = source_kernel.shape[2]
    window_rows = source_rows.shape[0]
    breadth = target_cols.shape[0]
    map_rows, _, features = source_features.shape
    rows = target_features.shape[0]
    span = rows + HALO
    width = -(-3 * window_rows * groups // LANES) * LANES
    chunk_rows = LANES // groups * span
    taps = 9 * groups
    hbm = pl.BlockSpec(memory_space=pltpu.HBM)
    operands = (
        source_rows,
        target_cols,
        target_features[:, 0],
        source_features[:, 0],
        target_kernel_one.reshape(taps, groups),
        source_kernel.reshape(taps, groups),
        target_kernel_two.reshape(taps, groups),
    )
    dma = pltpu.SemaphoreType.DMA
    out = pl.pallas_call(
        functools.partial(kernel, src_count, tgt_count, breadth, window_rows, groups),
        out_shape=jax.ShapeDtypeStruct((window_rows, rows, breadth * groups), BF16),
        in_specs=[hbm] * 7,
        out_specs=pl.BlockSpec(memory_space=pltpu.VMEM),
        scratch_shapes=[
            pltpu.SMEM((window_rows,), jnp.int32),
            pltpu.SMEM((breadth,), jnp.int32),
            pltpu.VMEM((breadth, span, features), BF16),
            pltpu.VMEM((3, map_rows, features), BF16),
            pltpu.VMEM((3, taps, groups), BF16),
            pltpu.VMEM(((breadth + 2) * span, width), BF16),
            pltpu.VMEM(((breadth + 2) * span, width), BF16),
            pltpu.VMEM((chunk_rows, LANES), F32),
            pltpu.VMEM((3, 3 * width, width), BF16),
            pltpu.VMEM((width, width), BF16),
            pltpu.VMEM((width, 3 * LANES), BF16),
            dma((7,)),
            dma((src_count,)),
            dma((src_count,)),
            dma((src_count,)),
            dma((src_count,)),
            dma((2,)),
            dma((2,)),
        ],
        compiler_params=pltpu.CompilerParams(
            collective_id=0, has_side_effects=True, vmem_limit_bytes=48 * 1024 * 1024
        ),
    )(*(pltpu.with_memory_space_constraint(operand, pltpu.HBM) for operand in operands))
    return out[:, None]


def solution(mesh):
    return jax.shard_map(
        functools.partial(local, mesh.shape["src"], mesh.shape["tgt"]),
        mesh=mesh,
        in_specs=(
            P("pair", "src", None),
            P(("pair", "tgt"), "src", None),
            P("pair"),
            P("pair"),
            P(),
            P(),
            P(),
        ),
        out_specs=P("pair", "src", "tgt", None),
        check_vma=False,
    )
```

profile of v0, /device:TPU:1, one launch (start us, length us, event | category | flops | bytes accessed | tf_op | source)
XLA Modules:
  0.0 13.3 jit_solution(13189938534290664110)
XLA Ops:
  0.0 12.6 %shard_map.73 = bf16[4,32,128]{2,1,0:T(8,128)(2,1)S(1)} custom-call(s32[4]{0:T(128)} %rows_hbm.1, s32[8]{0:T(128)} %cols_hbm.1, bf16[32,256]{1,0:T(8,128)(2,1)} %bitcast.12, bf16[32,256]{1,0:T(8,128)(2,1)} %bitcast.13, bf16[144,16]{1,0:T(8,128)(2,1)} %bitcast.9, bf16[144,16]{1,0:T(8,128)(2,1)} %bitcast.10, bf16[144,16]{1,0:T(8,128)(2,1)} %bitcast.11), custom_call_target="tpu_custom_call" | custom-call | tf_op jit(solution)/shard_map/pallas_call | solution.py:301
  12.6 0.6 %copy.10 = bf16[4,1,32,128]{3,2,1,0:T(8,128)(2,1)} copy(bf16[4,1,32,128]{3,2,1,0:T(8,128)(2,1)S(1)} %bitcast.8) | data formatting | bytes 65536
where the time goes:
time: 13.4 us; the launch traced here: 13.3 us
  Pallas kernels  12.6 us (94%)
  local copies, waits for them, and re-layouts  0.62 us (5%)
    pallas_call x1, Pallas kernels, local(): pl.pallas_call(functools.partial(kernel, src_count, tgt_count, breadth, w...  12.6 us
    unnamed x1, local copies, waits for them, and re-layouts  0.62 us

commit v1 on v0

--- a/solution.py
+++ b/solution.py
@@ -42,6 +42,9 @@
     sbuf,
     taps,
     vol,
+    rim,
+    edges,
+    acc,
     sec,
     stage,
     w1,
@@ -59,7 +62,7 @@
     map_rows = src_hbm.shape[0]
     channels = features // groups
     span = rows + HALO
-    width = vol.shape[1]
+    width = vol.shape[2]
     column_lanes = window_rows * groups
     per_block = LANES // groups
     chunks = breadth // per_block
@@ -78,7 +81,7 @@
         pl.semaphore_signal(barrier, inc=1, device_id={"tgt": 1 - half}, device_id_type=MESH)
 
     own = [
-        pltpu.make_async_copy(tgt_hbm, buf.at[me, main], local_sem.at[0]),
+        pltpu.make_async_copy(tgt_hbm, buf.at[me], local_sem.at[0]),
         pltpu.make_async_copy(src_hbm, sbuf.at[1], local_sem.at[1]),
         pltpu.make_async_copy(k1_hbm, taps.at[0], local_sem.at[2]),
         pltpu.make_async_copy(ks_hbm, taps.at[1], local_sem.at[3]),
@@ -90,8 +93,8 @@
         copy.start()
     pl.semaphore_wait(barrier, src_count - 1 + (1 if tgt_count > 1 else 0))
 
-    edge = pl.ds(pl.multiple_of(half * HALO + (1 - half) * (rows - HALO), HALO), HALO)
-    landing = pl.ds(pl.multiple_of(half * rows, HALO), HALO)
+    edge = pl.ds(pl.multiple_of((1 - half) * (rows - HALO), HALO), HALO)
+    arrived = pl.ds(pl.multiple_of((1 - half) * rows, HALO), HALO)
 
     to_right = pltpu.make_async_remote_copy(
         src_ref=src_hbm, dst_ref=sbuf.at[0], send_sem=src_send.at[0], recv_sem=src_recv.at[0],
@@ -105,7 +108,7 @@
     for d in range(1, src_count):
         sends.append(
             pltpu.make_async_remote_copy(
-                src_ref=tgt_hbm, dst_ref=buf.at[me, main], send_sem=send_sem.at[d],
+                src_ref=tgt_hbm, dst_ref=buf.at[me], send_sem=send_sem.at[d],
                 recv_sem=recv_sem.at[d], device_id={"src": peer(d)}, device_id_type=MESH,
             )
         )
@@ -115,23 +118,19 @@
     for d in order:
         sends[d - 1].start()
 
-    def forward(d, source):
-        column = lax.rem(me + src_count - d, src_count)
-        return pltpu.make_async_remote_copy(
-            src_ref=source(column), dst_ref=buf.at[column, landing], send_sem=halo_send.at[d],
-            recv_sem=halo_recv.at[d], device_id={"tgt": 1 - half}, device_id_type=MESH,
-        )
-
-    forwards = []
-    if tgt_count > 1:
-        offset = pl.multiple_of((1 - half) * (rows - HALO), HALO)
-        forwards.append(forward(0, lambda column: tgt_hbm.at[pl.ds(offset, HALO)]))
-        forwards[0].start()
+    exchange = pltpu.make_async_remote_copy(
+        src_ref=edges, dst_ref=rim.at[pl.ds(0, breadth)], send_sem=halo_send.at[0],
+        recv_sem=halo_recv.at[0], device_id={"tgt": 1 - half}, device_id_type=MESH,
+    )
 
     zero_block = jnp.zeros((span, width), BF16)
-    for ref in (vol, sec):
-        ref[pl.ds(0, span), :] = zero_block
-        ref[pl.ds((breadth + 1) * span, span), :] = zero_block
+    vol[breadth] = zero_block[:rows]
+    rim[breadth] = zero_block[:HALO]
+    if tgt_count == 1:
+        for column in range(breadth):
+            rim[column] = zero_block[:HALO]
+    sec[pl.ds(0, span), :] = zero_block
+    sec[pl.ds((breadth + 1) * span, span), :] = zero_block
     for copy in own[2:5]:
         copy.wait()
     expand = (iota((groups, width), 1) % groups == iota((groups, width), 0)).astype(BF16)
@@ -193,26 +192,46 @@
         parts.append(jnp.zeros((width - 3 * column_lanes, features), BF16))
     weights = jnp.concatenate(parts, axis=0)
 
+    position = iota((HALO, width), 0)
+    first_kept = (1 - half) * (HALO - 2)
+    kept = (position >= first_kept) & (position < first_kept + 2)
+
+    def score(column):
+        scores = lax.dot_general(
+            buf[column], weights, (((1,), (1,)), ((), ())), preferred_element_type=F32
+        ) * (channels ** -0.5)
+        vol[column] = scores.astype(BF16)
+        if tgt_count > 1:
+            edges[column] = jnp.where(kept, vol[column, edge, :], zero_block[:HALO])
+
     own[0].wait()
-    for d in range(1, src_count):
+    score(me)
+    for d in reversed(order):
         sends[d - 1].wait_recv()
-        if tgt_count > 1:
-            copy = forward(d, lambda column: buf.at[column, edge])
-            copy.start()
-            forwards.append(copy)
-    for copy in forwards:
-        copy.wait_recv()
-
-    def volume_chunk(chunk):
-        window = jnp.concatenate(
-            [buf[cols_ref[chunk * per_block + i]] for i in range(per_block)], axis=0
-        )
-        scores = lax.dot_general(
-            window, weights, (((1,), (1,)), ((), ())), preferred_element_type=F32
-        ) * (channels ** -0.5)
-        vol[pl.ds(pl.multiple_of((chunk * per_block + 1) * span, span), chunk_rows), :] = (
-            jnp.where(valid(2), scores, 0.0).astype(BF16)
-        )
+        score(lax.rem(me + src_count - d, src_count))
+    if tgt_count > 1:
+        exchange.start()
+
+    def gather(chunk, held):
+        taps_of_row = []
+        for b in range(3):
+            blocks = []
+            for i in range(per_block):
+                spot = chunk * per_block + i + b - 1
+                inside = (spot >= 0) & (spot < breadth)
+                known = cols_ref[jnp.clip(spot, 0, breadth - 1)]
+                blocks.append(held[jnp.where(inside, known, breadth)])
+            taps_of_row.append(jnp.concatenate(blocks, axis=0))
+        return jnp.concatenate(taps_of_row, axis=1)
+
+    def first_part(chunk, held, place):
+        window = gather(chunk, held)
+        home = pl.ds(pl.multiple_of(chunk * per_block, per_block), per_block)
+        for a in range(3):
+            acc[a, home, place, :] = dot(window, w1[a]).reshape(per_block, -1, width)
+
+    def main_chunk(chunk):
+        first_part(chunk, vol, main)
 
     def at(chunk, b):
         return pl.ds(pl.multiple_of((chunk * per_block + b) * span, span), chunk_rows)
@@ -222,8 +241,9 @@
         return total + pltpu.roll(parts[2], chunk_rows - 1, 0)
 
     def middle_chunk(chunk):
-        window = jnp.concatenate([vol[at(chunk, b), :] for b in range(3)], axis=1)
-        one = shifted([dot(window, w1[a]) for a in range(3)])
+        first_part(chunk, rim, arrived)
+        home = pl.ds(pl.multiple_of(chunk * per_block, per_block), per_block)
+        one = shifted([acc[a, home].reshape(chunk_rows, width) for a in range(3)])
         one = jnp.maximum(one, 0.0).astype(BF16)
         two = jnp.maximum(dot(one, w2[...]), 0.0)
         sec[at(chunk, 1), :] = jnp.where(valid(1), two, 0.0).astype(BF16)
@@ -255,7 +275,9 @@
                 total = jnp.where((group - h) % window_rows == d, rolled[d], total)
             out_ref[h, :, pl.ds(pl.multiple_of(chunk * LANES, LANES), LANES)] = total.astype(BF16)
 
-    for step in (volume_chunk, middle_chunk, last_chunk):
+    for step in (main_chunk, middle_chunk, last_chunk):
+        if step is middle_chunk and tgt_count > 1:
+            exchange.wait_recv()
         if chunks == 1:
             step(0)
         else:
@@ -263,8 +285,8 @@
 
     for copy in sends:
         copy.wait_send()
-    for copy in forwards:
-        copy.wait_send()
+    if tgt_count > 1:
+        exchange.wait_send()
 
 
 def local(
@@ -306,10 +328,13 @@
         scratch_shapes=[
             pltpu.SMEM((window_rows,), jnp.int32),
             pltpu.SMEM((breadth,), jnp.int32),
-            pltpu.VMEM((breadth, span, features), BF16),
+            pltpu.VMEM((breadth, rows, features), BF16),
             pltpu.VMEM((3, map_rows, features), BF16),
             pltpu.VMEM((3, taps, groups), BF16),
-            pltpu.VMEM(((breadth + 2) * span, width), BF16),
+            pltpu.VMEM((breadth + 1, rows, width), BF16),
+            pltpu.VMEM((breadth + 1, HALO, width), BF16),
+            pltpu.VMEM((breadth, HALO, width), BF16),
+            pltpu.VMEM((3, breadth, span, width), F32),
             pltpu.VMEM(((breadth + 2) * span, width), BF16),
             pltpu.VMEM((chunk_rows, LANES), F32),
             pltpu.VMEM((3, 3 * width, width), BF16),
@@ -318,8 +343,8 @@
             dma((7,)),
             dma((src_count,)),
             dma((src_count,)),
-            dma((src_count,)),
-            dma((src_count,)),
+            dma((1,)),
+            dma((1,)),
             dma((2,)),
             dma((2,)),
         ],

time: 13.4 us -> 13.8 us (1.030)
  Pallas kernels: 12.6 us -> 13 us
    pallas_call x1, Pallas kernels: 12.6 us -> 13 us  [local(): pl.pallas_call(functools.partial(kernel, src_count, tgt_count, breadth, w...]
where the time goes in v1:
time: 13.8 us; the launch traced here: 13.7 us
  Pallas kernels  13 us (94%)
  local copies, waits for them, and re-layouts  0.62 us (4%)
    pallas_call x1, Pallas kernels, local(): pl.pallas_call(functools.partial(kernel, src_count, tgt_count, breadth, w...  13 us
    unnamed x1, local copies, waits for them, and re-layouts  0.62 us

profile of v1, /device:TPU:1, one launch (start us, length us, event | category | flops | bytes accessed | tf_op | source)
XLA Modules:
  0.0 13.7 jit_solution(12544757003393418758)
XLA Ops:
  0.0 13.0 %shard_map.73 = bf16[4,32,128]{2,1,0:T(8,128)(2,1)S(1)} custom-call(s32[4]{0:T(128)} %rows_hbm.1, s32[8]{0:T(128)} %cols_hbm.1, bf16[32,256]{1,0:T(8,128)(2,1)} %bitcast.12, bf16[32,256]{1,0:T(8,128)(2,1)} %bitcast.13, bf16[144,16]{1,0:T(8,128)(2,1)} %bitcast.9, bf16[144,16]{1,0:T(8,128)(2,1)} %bitcast.10, bf16[144,16]{1,0:T(8,128)(2,1)} %bitcast.11), custom_call_target="tpu_custom_call" | custom-call | tf_op jit(solution)/shard_map/pallas_call | solution.py:323
  13.1 0.6 %copy.10 = bf16[4,1,32,128]{3,2,1,0:T(8,128)(2,1)} copy(bf16[4,1,32,128]{3,2,1,0:T(8,128)(2,1)S(1)} %bitcast.8) | data formatting | bytes 65536

commit v2 on v0

--- a/solution.py
+++ b/solution.py
@@ -16,6 +16,14 @@
 
 def iota(shape, dim):
     return lax.broadcasted_iota(jnp.int32, shape, dim)
+
+
+def quotient(x, n):
+    return x >> (n.bit_length() - 1) if n & (n - 1) == 0 else x // n
+
+
+def remainder(x, n):
+    return x & (n - 1) if n & (n - 1) == 0 else x % n
 
 
 def dot(a, b):
@@ -59,7 +67,7 @@
     map_rows = src_hbm.shape[0]
     channels = features // groups
     span = rows + HALO
-    width = vol.shape[1]
+    width = vol.shape[2]
     column_lanes = window_rows * groups
     per_block = LANES // groups
     chunks = breadth // per_block
@@ -129,14 +137,16 @@
         forwards[0].start()
 
     zero_block = jnp.zeros((span, width), BF16)
-    for ref in (vol, sec):
-        ref[pl.ds(0, span), :] = zero_block
-        ref[pl.ds((breadth + 1) * span, span), :] = zero_block
+    vol[0] = zero_block
+    vol[breadth + 1] = zero_block
+    sec[1] = zero_block
+    sec[breadth] = zero_block
     for copy in own[2:5]:
         copy.wait()
-    expand = (iota((groups, width), 1) % groups == iota((groups, width), 0)).astype(BF16)
+    expand = (remainder(iota((groups, width), 1), groups) == iota((groups, width), 0)).astype(BF16)
     spread = [dot(taps[i], expand).astype(BF16) for i in range(3)]
-    lane_group = iota((groups, width), 1) // groups
+    lane_group = quotient(iota((groups, width), 1), groups)
+    lane_row = remainder(lane_group, window_rows)
     nothing = jnp.zeros((groups, width), BF16)
 
     def tap(i, a, b):
@@ -155,31 +165,34 @@
         three = [nothing[:, :LANES]] * 3
         if k < 3:
             for a in range(3):
-                two = jnp.where(lane_group % window_rows == h - a + 1, tap(1, a, k), two)
+                two = jnp.where(lane_row == h - a + 1, tap(1, a, k), two)
                 three[a] = jnp.where(
-                    (lane_group % window_rows == h)[:, :LANES], tap(2, a, k)[:, :LANES], three[a]
+                    (lane_row == h)[:, :LANES], tap(2, a, k)[:, :LANES], three[a]
                 )
         w2[pl.ds(j * groups, groups), :] = two
         for a in range(3):
             w3[pl.ds(j * groups, groups), pl.ds(a * LANES, LANES)] = three[a]
 
     def valid(extra):
-        position = iota((chunk_rows, width), 0) % span
+        position = iota((span, width), 0)
         low = half * (HALO - extra)
-        return (position >= low) & (position < low + rows + extra)
+        return ((position >= low) & (position < low + rows + extra))[None]
+
+    valid_one, valid_two = valid(2), valid(1)
 
     own[1].wait()
     own[5].wait()
     own[6].wait()
     to_right.wait()
     to_left.wait()
-    row_of = iota((column_lanes, map_rows), 0) // groups
+    row_of = quotient(iota((column_lanes, map_rows), 0), groups)
     wanted = jnp.zeros((column_lanes, map_rows), jnp.int32)
     for h in range(window_rows):
         wanted = jnp.where(row_of == h, rows_ref[h], wanted)
     select = (iota((column_lanes, map_rows), 1) == wanted).astype(BF16)
     same_group = (
-        iota((column_lanes, features), 1) // channels == iota((column_lanes, features), 0) % groups
+        quotient(iota((column_lanes, features), 1), channels)
+        == remainder(iota((column_lanes, features), 0), groups)
     )
     parts = []
     for k in range(3):
@@ -210,50 +223,50 @@
         scores = lax.dot_general(
             window, weights, (((1,), (1,)), ((), ())), preferred_element_type=F32
         ) * (channels ** -0.5)
-        vol[pl.ds(pl.multiple_of((chunk * per_block + 1) * span, span), chunk_rows), :] = (
-            jnp.where(valid(2), scores, 0.0).astype(BF16)
-        )
-
-    def at(chunk, b):
-        return pl.ds(pl.multiple_of((chunk * per_block + b) * span, span), chunk_rows)
+        vol[pl.ds(chunk * per_block + 1, per_block)] = jnp.where(
+            valid_one, scores.reshape(per_block, span, width), 0.0
+        ).astype(BF16)
+
+    def at(ref, chunk, b):
+        return ref[pl.ds(chunk * per_block + b, per_block)].reshape(chunk_rows, width)
 
     def shifted(parts):
         total = parts[1] + pltpu.roll(parts[0], 1, 0)
         return total + pltpu.roll(parts[2], chunk_rows - 1, 0)
 
     def middle_chunk(chunk):
-        window = jnp.concatenate([vol[at(chunk, b), :] for b in range(3)], axis=1)
+        window = jnp.concatenate([at(vol, chunk, b) for b in range(3)], axis=1)
         one = shifted([dot(window, w1[a]) for a in range(3)])
         one = jnp.maximum(one, 0.0).astype(BF16)
-        two = jnp.maximum(dot(one, w2[...]), 0.0)
-        sec[at(chunk, 1), :] = jnp.where(valid(1), two, 0.0).astype(BF16)
+        two = jnp.maximum(dot(one, w2[...]), 0.0).reshape(per_block, span, width)
+        two = jnp.where(valid_two, two, 0.0).astype(BF16)
+        for b in range(3):
+            lanes = slice(b * column_lanes, (b + 1) * column_lanes if b < 2 else width)
+            sec[pl.ds(chunk * per_block + 2 - b, per_block), :, lanes] = two[:, :, lanes]
 
     def last_chunk(chunk):
-        which = iota((chunk_rows, width), 1) // column_lanes
-        window = jnp.where(
-            which == 0,
-            sec[at(chunk, 0), :],
-            jnp.where(which == 1, sec[at(chunk, 1), :], sec[at(chunk, 2), :]),
-        )
-        three = dot(window, w3[...])
+        three = dot(at(sec, chunk, 1), w3[...])
         three = shifted([three[:, a * LANES : (a + 1) * LANES] for a in range(3)])
         stage[...] = jnp.maximum(three, 0.0)
         pieces = [
             stage[pl.ds(pl.multiple_of(i * span + half * HALO, HALO), rows), :]
             for i in range(per_block)
         ]
-        group = iota((rows, LANES), 1) // groups
         rolled = []
         for d in range(window_rows):
             mixed = pieces[d % per_block]
             for j in range(1, per_block):
-                mixed = jnp.where(group == j, pieces[(j + d) % per_block], mixed)
+                mixed = jnp.where(in_group[j], pieces[(j + d) % per_block], mixed)
             rolled.append(pltpu.roll(mixed, d * groups, 1) if d else mixed)
         for h in range(window_rows):
             total = rolled[0]
             for d in range(1, window_rows):
-                total = jnp.where((group - h) % window_rows == d, rolled[d], total)
+                total = jnp.where(in_row[(d + h) % window_rows], rolled[d], total)
             out_ref[h, :, pl.ds(pl.multiple_of(chunk * LANES, LANES), LANES)] = total.astype(BF16)
+
+    group = quotient(iota((rows, LANES), 1), groups)
+    in_group = [group == j for j in range(per_block)]
+    in_row = [remainder(group, window_rows) == h for h in range(window_rows)]
 
     for step in (volume_chunk, middle_chunk, last_chunk):
         if chunks == 1:
@@ -309,8 +322,8 @@
             pltpu.VMEM((breadth, span, features), BF16),
             pltpu.VMEM((3, map_rows, features), BF16),
             pltpu.VMEM((3, taps, groups), BF16),
-            pltpu.VMEM(((breadth + 2) * span, width), BF16),
-            pltpu.VMEM(((breadth + 2) * span, width), BF16),
+            pltpu.VMEM((breadth + 2, span, width), BF16),
+            pltpu.VMEM((breadth + 2, span, width), BF16),
             pltpu.VMEM((chunk_rows, LANES), F32),
             pltpu.VMEM((3, 3 * width, width), BF16),
             pltpu.VMEM((width, width), BF16),

time: 13.4 us -> 13.4 us (level)
  no operation moved by 1% of the time
where the time goes in v2:
time: 13.4 us; the launch traced here: 13.3 us
  Pallas kernels  12.7 us (95%)
  local copies, waits for them, and re-layouts  0.62 us (5%)
    pallas_call x1, Pallas kernels, local(): pl.pallas_call(functools.partial(kernel, src_count, tgt_count, breadth, w...  12.7 us
    unnamed x1, local copies, waits for them, and re-layouts  0.62 us

profile of v2, /device:TPU:1, one launch (start us, length us, event | category | flops | bytes accessed | tf_op | source)
XLA Modules:
  0.0 13.3 jit_solution(18029983309486745189)
XLA Ops:
  0.0 12.7 %shard_map.73 = bf16[4,32,128]{2,1,0:T(8,128)(2,1)S(1)} custom-call(s32[4]{0:T(128)} %rows_hbm.1, s32[8]{0:T(128)} %cols_hbm.1, bf16[32,256]{1,0:T(8,128)(2,1)} %bitcast.12, bf16[32,256]{1,0:T(8,128)(2,1)} %bitcast.13, bf16[144,16]{1,0:T(8,128)(2,1)} %bitcast.9, bf16[144,16]{1,0:T(8,128)(2,1)} %bitcast.10, bf16[144,16]{1,0:T(8,128)(2,1)} %bitcast.11), custom_call_target="tpu_custom_call" | custom-call | tf_op jit(solution)/shard_map/pallas_call | solution.py:314
  12.7 0.6 %copy.10 = bf16[4,1,32,128]{3,2,1,0:T(8,128)(2,1)} copy(bf16[4,1,32,128]{3,2,1,0:T(8,128)(2,1)S(1)} %bitcast.8) | data formatting | bytes 65536

commit v3 on v2

--- a/solution.py
+++ b/solution.py
@@ -47,9 +47,12 @@
     rows_ref,
     cols_ref,
     buf,
+    src_map,
     sbuf,
     taps,
+    rim,
     vol,
+    acc,
     sec,
     stage,
     w1,
@@ -79,6 +82,8 @@
     def peer(d):
         return lax.rem(me + d, src_count)
 
+    sbuf[0] = jnp.zeros(sbuf.shape[1:], BF16)
+    sbuf[2] = jnp.zeros(sbuf.shape[1:], BF16)
     barrier = pltpu.get_barrier_semaphore()
     for d in range(1, src_count):
         pl.semaphore_signal(barrier, inc=1, device_id={"src": peer(d)}, device_id_type=MESH)
@@ -86,8 +91,8 @@
         pl.semaphore_signal(barrier, inc=1, device_id={"tgt": 1 - half}, device_id_type=MESH)
 
     own = [
-        pltpu.make_async_copy(tgt_hbm, buf.at[me, main], local_sem.at[0]),
-        pltpu.make_async_copy(src_hbm, sbuf.at[1], local_sem.at[1]),
+        pltpu.make_async_copy(tgt_hbm, buf.at[me], local_sem.at[0]),
+        pltpu.make_async_copy(src_hbm, src_map, local_sem.at[1]),
         pltpu.make_async_copy(k1_hbm, taps.at[0], local_sem.at[2]),
         pltpu.make_async_copy(ks_hbm, taps.at[1], local_sem.at[3]),
         pltpu.make_async_copy(k2_hbm, taps.at[2], local_sem.at[4]),
@@ -98,43 +103,58 @@
         copy.start()
     pl.semaphore_wait(barrier, src_count - 1 + (1 if tgt_count > 1 else 0))
 
-    edge = pl.ds(pl.multiple_of(half * HALO + (1 - half) * (rows - HALO), HALO), HALO)
-    landing = pl.ds(pl.multiple_of(half * rows, HALO), HALO)
+    edge = pl.ds(pl.multiple_of((1 - half) * (rows - HALO), HALO), HALO)
+    arrived = pl.ds(pl.multiple_of((1 - half) * rows, HALO), HALO)
 
     to_right = pltpu.make_async_remote_copy(
-        src_ref=src_hbm, dst_ref=sbuf.at[0], send_sem=src_send.at[0], recv_sem=src_recv.at[0],
+        src_ref=sbuf.at[1], dst_ref=sbuf.at[0], send_sem=src_send.at[0], recv_sem=src_recv.at[0],
         device_id={"src": lax.rem(me + 1, src_count)}, device_id_type=MESH,
     )
     to_left = pltpu.make_async_remote_copy(
-        src_ref=src_hbm, dst_ref=sbuf.at[2], send_sem=src_send.at[1], recv_sem=src_recv.at[1],
+        src_ref=sbuf.at[1], dst_ref=sbuf.at[2], send_sem=src_send.at[1], recv_sem=src_recv.at[1],
         device_id={"src": lax.rem(me + src_count - 1, src_count)}, device_id_type=MESH,
     )
     sends = []
     for d in range(1, src_count):
         sends.append(
             pltpu.make_async_remote_copy(
-                src_ref=tgt_hbm, dst_ref=buf.at[me, main], send_sem=send_sem.at[d],
+                src_ref=tgt_hbm, dst_ref=buf.at[me], send_sem=send_sem.at[d],
                 recv_sem=recv_sem.at[d], device_id={"src": peer(d)}, device_id_type=MESH,
             )
         )
     order = sorted(range(1, src_count), key=lambda d: -min(d, src_count - d))
-    to_right.start()
-    to_left.start()
     for d in order:
         sends[d - 1].start()
 
     def forward(d, source):
         column = lax.rem(me + src_count - d, src_count)
         return pltpu.make_async_remote_copy(
-            src_ref=source(column), dst_ref=buf.at[column, landing], send_sem=halo_send.at[d],
+            src_ref=source(column), dst_ref=rim.at[column], send_sem=halo_send.at[d],
             recv_sem=halo_recv.at[d], device_id={"tgt": 1 - half}, device_id_type=MESH,
         )
 
     forwards = []
-    if tgt_count > 1:
+    if tgt_count == 1:
+        for column in range(breadth):
+            rim[column] = jnp.zeros((HALO, features), BF16)
+    else:
         offset = pl.multiple_of((1 - half) * (rows - HALO), HALO)
         forwards.append(forward(0, lambda column: tgt_hbm.at[pl.ds(offset, HALO)]))
         forwards[0].start()
+
+    has_left, has_right = me > 0, me < src_count - 1
+    own[1].wait()
+    own[5].wait()
+    own[6].wait()
+    picked = sbuf.shape[1]
+    row_of = iota((picked, map_rows), 0)
+    wanted = jnp.full((picked, map_rows), -1, jnp.int32)
+    for h in range(window_rows):
+        wanted = jnp.where(row_of == h, rows_ref[h], wanted)
+    choice = (iota((picked, map_rows), 1) == wanted).astype(BF16)
+    sbuf[1] = dot(choice, src_map[...]).astype(BF16)
+    pl.when(has_right)(to_right.start)
+    pl.when(has_left)(to_left.start)
 
     zero_block = jnp.zeros((span, width), BF16)
     vol[0] = zero_block
@@ -178,18 +198,16 @@
         low = half * (HALO - extra)
         return ((position >= low) & (position < low + rows + extra))[None]
 
-    valid_one, valid_two = valid(2), valid(1)
-
-    own[1].wait()
-    own[5].wait()
-    own[6].wait()
-    to_right.wait()
-    to_left.wait()
-    row_of = quotient(iota((column_lanes, map_rows), 0), groups)
-    wanted = jnp.zeros((column_lanes, map_rows), jnp.int32)
-    for h in range(window_rows):
-        wanted = jnp.where(row_of == h, rows_ref[h], wanted)
-    select = (iota((column_lanes, map_rows), 1) == wanted).astype(BF16)
+    valid_two = valid(1)
+    first_kept = half * (HALO - 2)
+    rim_position = iota((HALO, width), 0)
+    in_rim = ((rim_position >= first_kept) & (rim_position < first_kept + 2))[None]
+
+    pl.when(has_left)(to_right.wait_recv)
+    pl.when(has_right)(to_left.wait_recv)
+    select = (
+        quotient(iota((column_lanes, picked), 0), groups) == iota((column_lanes, picked), 1)
+    ).astype(BF16)
     same_group = (
         quotient(iota((column_lanes, features), 1), channels)
         == remainder(iota((column_lanes, features), 0), groups)
@@ -213,19 +231,39 @@
             copy = forward(d, lambda column: buf.at[column, edge])
             copy.start()
             forwards.append(copy)
-    for copy in forwards:
-        copy.wait_recv()
-
-    def volume_chunk(chunk):
-        window = jnp.concatenate(
-            [buf[cols_ref[chunk * per_block + i]] for i in range(per_block)], axis=0
-        )
+    def volume(chunk, place, keep):
+        spots = [cols_ref[chunk * per_block + i] for i in range(per_block)]
+        held, spot_rows = (buf, rows) if place is main else (rim, HALO)
+        window = jnp.concatenate([held[spot] for spot in spots], axis=0)
         scores = lax.dot_general(
             window, weights, (((1,), (1,)), ((), ())), preferred_element_type=F32
         ) * (channels ** -0.5)
-        vol[pl.ds(chunk * per_block + 1, per_block)] = jnp.where(
-            valid_one, scores.reshape(per_block, span, width), 0.0
-        ).astype(BF16)
+        scores = scores.reshape(per_block, spot_rows, width)
+        if keep is not None:
+            scores = jnp.where(keep, scores, 0.0)
+        vol[pl.ds(chunk * per_block + 1, per_block), place, :] = scores.astype(BF16)
+
+    def sums(chunk, place):
+        window = jnp.concatenate(
+            [
+                vol[pl.ds(chunk * per_block + b, per_block), place, :].reshape(-1, width)
+                for b in range(3)
+            ],
+            axis=1,
+        )
+        for a in range(3):
+            acc[a, pl.ds(chunk * per_block, per_block), place, :] = dot(window, w1[a]).reshape(
+                per_block, -1, width
+            )
+
+    def main_volume(chunk):
+        volume(chunk, main, None)
+
+    def main_sums(chunk):
+        sums(chunk, main)
+
+    def rim_volume(chunk):
+        volume(chunk, arrived, in_rim)
 
     def at(ref, chunk, b):
         return ref[pl.ds(chunk * per_block + b, per_block)].reshape(chunk_rows, width)
@@ -235,8 +273,8 @@
         return total + pltpu.roll(parts[2], chunk_rows - 1, 0)
 
     def middle_chunk(chunk):
-        window = jnp.concatenate([at(vol, chunk, b) for b in range(3)], axis=1)
-        one = shifted([dot(window, w1[a]) for a in range(3)])
+        sums(chunk, arrived)
+        one = shifted([at(acc.at[a], chunk, 0) for a in range(3)])
         one = jnp.maximum(one, 0.0).astype(BF16)
         two = jnp.maximum(dot(one, w2[...]), 0.0).reshape(per_block, span, width)
         two = jnp.where(valid_two, two, 0.0).astype(BF16)
@@ -268,12 +306,17 @@
     in_group = [group == j for j in range(per_block)]
     in_row = [remainder(group, window_rows) == h for h in range(window_rows)]
 
-    for step in (volume_chunk, middle_chunk, last_chunk):
+    for step in (main_volume, main_sums, rim_volume, middle_chunk, last_chunk):
+        if step is rim_volume:
+            for copy in forwards:
+                copy.wait_recv()
         if chunks == 1:
             step(0)
         else:
             pl.loop(0, chunks)(step)
 
+    pl.when(has_right)(to_right.wait_send)
+    pl.when(has_left)(to_left.wait_send)
     for copy in sends:
         copy.wait_send()
     for copy in forwards:
@@ -319,10 +362,13 @@
         scratch_shapes=[
             pltpu.SMEM((window_rows,), jnp.int32),
             pltpu.SMEM((breadth,), jnp.int32),
-            pltpu.VMEM((breadth, span, features), BF16),
-            pltpu.VMEM((3, map_rows, features), BF16),
+            pltpu.VMEM((breadth, rows, features), BF16),
+            pltpu.VMEM((map_rows, features), BF16),
+            pltpu.VMEM((3, -(-window_rows // 16) * 16, features), BF16),
             pltpu.VMEM((3, taps, groups), BF16),
+            pltpu.VMEM((breadth, HALO, features), BF16),
             pltpu.VMEM((breadth + 2, span, width), BF16),
+            pltpu.VMEM((3, breadth, span, width), F32),
             pltpu.VMEM((breadth + 2, span, width), BF16),
             pltpu.VMEM((chunk_rows, LANES), F32),
             pltpu.VMEM((3, 3 * width, width), BF16),

time: 13.4 us -> 12.7 us (0.948)
  Pallas kernels: 12.7 us -> 11.9 us
    pallas_call x1, Pallas kernels: 12.7 us -> 11.9 us  [local(): pl.pallas_call(functools.partial(kernel, src_count, tgt_count, breadth, w...]
where the time goes in v3:
time: 12.7 us; the launch traced here: 12.5 us
  Pallas kernels  11.9 us (94%)
  local copies, waits for them, and re-layouts  0.62 us (5%)
    pallas_call x1, Pallas kernels, local(): pl.pallas_call(functools.partial(kernel, src_count, tgt_count, breadth, w...  11.9 us
    unnamed x1, local copies, waits for them, and re-layouts  0.62 us

profile of v3, /device:TPU:1, one launch (start us, length us, event | category | flops | bytes accessed | tf_op | source)
XLA Modules:
  0.0 12.5 jit_solution(5662768634657898908)
XLA Ops:
  0.0 11.9 %shard_map.73 = bf16[4,32,128]{2,1,0:T(8,128)(2,1)S(1)} custom-call(s32[4]{0:T(128)} %rows_hbm.1, s32[8]{0:T(128)} %cols_hbm.1, bf16[32,256]{1,0:T(8,128)(2,1)} %bitcast.12, bf16[32,256]{1,0:T(8,128)(2,1)} %bitcast.13, bf16[144,16]{1,0:T(8,128)(2,1)} %bitcast.9, bf16[144,16]{1,0:T(8,128)(2,1)} %bitcast.10, bf16[144,16]{1,0:T(8,128)(2,1)} %bitcast.11), custom_call_target="tpu_custom_call" | custom-call | tf_op jit(solution)/shard_map/pallas_call | solution.py:357
  11.9 0.6 %copy.10 = bf16[4,1,32,128]{3,2,1,0:T(8,128)(2,1)} copy(bf16[4,1,32,128]{3,2,1,0:T(8,128)(2,1)S(1)} %bitcast.8) | data formatting | bytes 65536

commit v4 on v3

--- a/solution.py
+++ b/solution.py
@@ -61,6 +61,8 @@
     local_sem,
     send_sem,
     recv_sem,
+    relay_send,
+    relay_recv,
     halo_send,
     halo_recv,
     src_send,
@@ -79,14 +81,32 @@
     half = lax.axis_index("tgt")
     main = pl.ds(pl.multiple_of(half * HALO, HALO), rows)
 
+    lines = src_count // 2
+    side = lax.rem(me, 2)
+    rank = me // 2
+    mate = me + 1 - 2 * side
+    beyond = lax.rem(me + src_count - 1 + 2 * side, src_count)
+
     def peer(d):
-        return lax.rem(me + d, src_count)
+        if lines & (lines - 1):
+            return lax.rem(rank + d, lines) * 2 + side
+        other = rank
+        for bit in range(d.bit_length()):
+            if d >> bit & 1:
+                other = other + (1 << bit) * (1 - 2 * lax.rem(rank // (1 << bit), 2))
+        return other * 2 + side
+
+    def sender(d):
+        if lines & (lines - 1):
+            return lax.rem(rank + lines - d, lines) * 2 + side
+        return peer(d)
 
     sbuf[0] = jnp.zeros(sbuf.shape[1:], BF16)
     sbuf[2] = jnp.zeros(sbuf.shape[1:], BF16)
     barrier = pltpu.get_barrier_semaphore()
-    for d in range(1, src_count):
-        pl.semaphore_signal(barrier, inc=1, device_id={"src": peer(d)}, device_id_type=MESH)
+    greeted = [peer(d) for d in range(1, lines)] + [mate, beyond]
+    for other in greeted:
+        pl.semaphore_signal(barrier, inc=1, device_id={"src": other}, device_id_type=MESH)
     if tgt_count > 1:
         pl.semaphore_signal(barrier, inc=1, device_id={"tgt": 1 - half}, device_id_type=MESH)
 
@@ -101,7 +121,7 @@
     ]
     for copy in own:
         copy.start()
-    pl.semaphore_wait(barrier, src_count - 1 + (1 if tgt_count > 1 else 0))
+    pl.semaphore_wait(barrier, len(greeted) + (1 if tgt_count > 1 else 0))
 
     edge = pl.ds(pl.multiple_of((1 - half) * (rows - HALO), HALO), HALO)
     arrived = pl.ds(pl.multiple_of((1 - half) * rows, HALO), HALO)
@@ -115,32 +135,36 @@
         device_id={"src": lax.rem(me + src_count - 1, src_count)}, device_id_type=MESH,
     )
     sends = []
-    for d in range(1, src_count):
+    for d in list(range(1, lines)) + [0]:
         sends.append(
             pltpu.make_async_remote_copy(
                 src_ref=tgt_hbm, dst_ref=buf.at[me], send_sem=send_sem.at[d],
-                recv_sem=recv_sem.at[d], device_id={"src": peer(d)}, device_id_type=MESH,
+                recv_sem=recv_sem.at[d], device_id={"src": peer(d) if d else mate},
+                device_id_type=MESH,
             )
         )
-    order = sorted(range(1, src_count), key=lambda d: -min(d, src_count - d))
-    for d in order:
-        sends[d - 1].start()
-
-    def forward(d, source):
-        column = lax.rem(me + src_count - d, src_count)
+    for copy in sends:
+        copy.start()
+
+    def forward(slot, column, source):
         return pltpu.make_async_remote_copy(
-            src_ref=source(column), dst_ref=rim.at[column], send_sem=halo_send.at[d],
-            recv_sem=halo_recv.at[d], device_id={"tgt": 1 - half}, device_id_type=MESH,
+            src_ref=source, dst_ref=rim.at[column], send_sem=halo_send.at[slot],
+            recv_sem=halo_recv.at[slot], device_id={"tgt": 1 - half}, device_id_type=MESH,
         )
 
     forwards = []
+
+    def pass_edge(slot, column, source):
+        if tgt_count > 1:
+            copy = forward(slot, column, source)
+            copy.start()
+            forwards.append(copy)
+
     if tgt_count == 1:
         for column in range(breadth):
             rim[column] = jnp.zeros((HALO, features), BF16)
-    else:
-        offset = pl.multiple_of((1 - half) * (rows - HALO), HALO)
-        forwards.append(forward(0, lambda column: tgt_hbm.at[pl.ds(offset, HALO)]))
-        forwards[0].start()
+    offset = pl.multiple_of((1 - half) * (rows - HALO), HALO)
+    pass_edge(0, me, tgt_hbm.at[pl.ds(offset, HALO)])
 
     has_left, has_right = me > 0, me < src_count - 1
     own[1].wait()
@@ -202,6 +226,20 @@
     first_kept = half * (HALO - 2)
     rim_position = iota((HALO, width), 0)
     in_rim = ((rim_position >= first_kept) & (rim_position < first_kept + 2))[None]
+
+    relays = []
+    for d in range(1, lines):
+        sends[d - 1].wait_recv()
+        column = sender(d)
+        relay = pltpu.make_async_remote_copy(
+            src_ref=buf.at[column], dst_ref=buf.at[column], send_sem=relay_send.at[d],
+            recv_sem=relay_recv.at[d], device_id={"src": mate}, device_id_type=MESH,
+        )
+        relay.start()
+        relays.append(relay)
+        pass_edge(d, column, buf.at[column, edge])
+    sends[-1].wait_recv()
+    pass_edge(lines, mate, buf.at[mate, edge])
 
     pl.when(has_left)(to_right.wait_recv)
     pl.when(has_right)(to_left.wait_recv)
@@ -225,12 +263,11 @@
     weights = jnp.concatenate(parts, axis=0)
 
     own[0].wait()
-    for d in range(1, src_count):
-        sends[d - 1].wait_recv()
-        if tgt_count > 1:
-            copy = forward(d, lambda column: buf.at[column, edge])
-            copy.start()
-            forwards.append(copy)
+    for d in range(1, lines):
+        relays[d - 1].wait_recv()
+        column = sender(d) + 1 - 2 * side
+        pass_edge(lines + d, column, buf.at[column, edge])
+
     def volume(chunk, place, keep):
         spots = [cols_ref[chunk * per_block + i] for i in range(per_block)]
         held, spot_rows = (buf, rows) if place is main else (rim, HALO)
@@ -317,7 +354,7 @@
 
     pl.when(has_right)(to_right.wait_send)
     pl.when(has_left)(to_left.wait_send)
-    for copy in sends:
+    for copy in sends + relays:
         copy.wait_send()
     for copy in forwards:
         copy.wait_send()
@@ -375,8 +412,10 @@
             pltpu.VMEM((width, width), BF16),
             pltpu.VMEM((width, 3 * LANES), BF16),
             dma((7,)),
-            dma((src_count,)),
-            dma((src_count,)),
+            dma((src_count // 2,)),
+            dma((src_count // 2,)),
+            dma((src_count // 2,)),
+            dma((src_count // 2,)),
             dma((src_count,)),
             dma((src_count,)),
             dma((2,)),

time: 12.7 us -> 14.2 us (1.12)
  Pallas kernels: 11.9 us -> 13.4 us
    pallas_call x1, Pallas kernels: 11.9 us -> 13.4 us  [local(): pl.pallas_call(functools.partial(kernel, src_count, tgt_count, breadth, w...]
where the time goes in v4:
time: 14.2 us; the launch traced here: 14.1 us
  Pallas kernels  13.4 us (94%)
  local copies, waits for them, and re-layouts  0.62 us (4%)
    pallas_call x1, Pallas kernels, local(): pl.pallas_call(functools.partial(kernel, src_count, tgt_count, breadth, w...  13.4 us
    unnamed x1, local copies, waits for them, and re-layouts  0.62 us

profile of v4, /device:TPU:1, one launch (start us, length us, event | category | flops | bytes accessed | tf_op | source)
XLA Modules:
  0.0 14.1 jit_solution(12590285884170312793)
XLA Ops:
  0.0 13.4 %shard_map.73 = bf16[4,32,128]{2,1,0:T(8,128)(2,1)S(1)} custom-call(s32[4]{0:T(128)} %rows_hbm.1, s32[8]{0:T(128)} %cols_hbm.1, bf16[32,256]{1,0:T(8,128)(2,1)} %bitcast.12, bf16[32,256]{1,0:T(8,128)(2,1)} %bitcast.13, bf16[144,16]{1,0:T(8,128)(2,1)} %bitcast.9, bf16[144,16]{1,0:T(8,128)(2,1)} %bitcast.10, bf16[144,16]{1,0:T(8,128)(2,1)} %bitcast.11), custom_call_target="tpu_custom_call" | custom-call | tf_op jit(solution)/shard_map/pallas_call | solution.py:394
  13.4 0.6 %copy.10 = bf16[4,1,32,128]{3,2,1,0:T(8,128)(2,1)} copy(bf16[4,1,32,128]{3,2,1,0:T(8,128)(2,1)S(1)} %bitcast.8) | data formatting | bytes 65536

commit v5 on v2

--- a/solution.py
+++ b/solution.py
@@ -79,11 +79,16 @@
     def peer(d):
         return lax.rem(me + d, src_count)
 
+    sbuf[0] = jnp.zeros(sbuf.shape[1:], BF16)
+    sbuf[2] = jnp.zeros(sbuf.shape[1:], BF16)
     barrier = pltpu.get_barrier_semaphore()
     for d in range(1, src_count):
         pl.semaphore_signal(barrier, inc=1, device_id={"src": peer(d)}, device_id_type=MESH)
     if tgt_count > 1:
-        pl.semaphore_signal(barrier, inc=1, device_id={"tgt": 1 - half}, device_id_type=MESH)
+        for d in range(src_count):
+            pl.semaphore_signal(
+                barrier, inc=1, device_id={"src": peer(d), "tgt": 1 - half}, device_id_type=MESH
+            )
 
     own = [
         pltpu.make_async_copy(tgt_hbm, buf.at[me, main], local_sem.at[0]),
@@ -96,9 +101,8 @@
     ]
     for copy in own:
         copy.start()
-    pl.semaphore_wait(barrier, src_count - 1 + (1 if tgt_count > 1 else 0))
-
-    edge = pl.ds(pl.multiple_of(half * HALO + (1 - half) * (rows - HALO), HALO), HALO)
+    pl.semaphore_wait(barrier, src_count - 1 + (src_count if tgt_count > 1 else 0))
+
     landing = pl.ds(pl.multiple_of(half * rows, HALO), HALO)
 
     to_right = pltpu.make_async_remote_copy(
@@ -118,23 +122,26 @@
             )
         )
     order = sorted(range(1, src_count), key=lambda d: -min(d, src_count - d))
-    to_right.start()
-    to_left.start()
+    has_left, has_right = me > 0, me < src_count - 1
+    pl.when(has_right)(to_right.start)
+    pl.when(has_left)(to_left.start)
+    offset = pl.multiple_of((1 - half) * (rows - HALO), HALO)
+    rims = []
+    if tgt_count > 1:
+        for d in range(src_count):
+            rims.append(
+                pltpu.make_async_remote_copy(
+                    src_ref=tgt_hbm.at[pl.ds(offset, HALO)], dst_ref=buf.at[me, landing],
+                    send_sem=halo_send.at[d], recv_sem=halo_recv.at[d],
+                    device_id={"src": peer(d), "tgt": 1 - half}, device_id_type=MESH,
+                )
+            )
     for d in order:
         sends[d - 1].start()
-
-    def forward(d, source):
-        column = lax.rem(me + src_count - d, src_count)
-        return pltpu.make_async_remote_copy(
-            src_ref=source(column), dst_ref=buf.at[column, landing], send_sem=halo_send.at[d],
-            recv_sem=halo_recv.at[d], device_id={"tgt": 1 - half}, device_id_type=MESH,
-        )
-
-    forwards = []
-    if tgt_count > 1:
-        offset = pl.multiple_of((1 - half) * (rows - HALO), HALO)
-        forwards.append(forward(0, lambda column: tgt_hbm.at[pl.ds(offset, HALO)]))
-        forwards[0].start()
+        if rims:
+            rims[d].start()
+    if rims:
+        rims[0].start()
 
     zero_block = jnp.zeros((span, width), BF16)
     vol[0] = zero_block
@@ -183,8 +190,8 @@
     own[1].wait()
     own[5].wait()
     own[6].wait()
-    to_right.wait()
-    to_left.wait()
+    pl.when(has_left)(to_right.wait_recv)
+    pl.when(has_right)(to_left.wait_recv)
     row_of = quotient(iota((column_lanes, map_rows), 0), groups)
     wanted = jnp.zeros((column_lanes, map_rows), jnp.int32)
     for h in range(window_rows):
@@ -207,13 +214,7 @@
     weights = jnp.concatenate(parts, axis=0)
 
     own[0].wait()
-    for d in range(1, src_count):
-        sends[d - 1].wait_recv()
-        if tgt_count > 1:
-            copy = forward(d, lambda column: buf.at[column, edge])
-            copy.start()
-            forwards.append(copy)
-    for copy in forwards:
+    for copy in sends + rims:
         copy.wait_recv()
 
     def volume_chunk(chunk):
@@ -274,9 +275,9 @@
         else:
             pl.loop(0, chunks)(step)
 
-    for copy in sends:
-        copy.wait_send()
-    for copy in forwards:
+    pl.when(has_right)(to_right.wait_send)
+    pl.when(has_left)(to_left.wait_send)
+    for copy in sends + rims:
         copy.wait_send()
 
 

time: 13.4 us -> 13.6 us (1.015)
  the two profiles are of different devices: /device:TPU:1 before, /device:TPU:0 now
where the time goes in v5:
time: 13.6 us; the launch traced here: 13.4 us
  Pallas kernels  12.8 us (94%)
  local copies, waits for them, and re-layouts  0.62 us (5%)
    pallas_call x1, Pallas kernels, local(): pl.pallas_call(functools.partial(kernel, src_count, tgt_count, breadth, w...  12.8 us
    unnamed x1, local copies, waits for them, and re-layouts  0.62 us

profile of v5, /device:TPU:0, one launch (start us, length us, event | category | flops | bytes accessed | tf_op | source)
XLA Modules:
  0.0 13.4 jit_solution(12769105236685806132)
XLA Ops:
  0.0 12.8 %shard_map.73 = bf16[4,32,128]{2,1,0:T(8,128)(2,1)S(1)} custom-call(s32[4]{0:T(128)} %rows_hbm.1, s32[8]{0:T(128)} %cols_hbm.1, bf16[32,256]{1,0:T(8,128)(2,1)} %bitcast.12, bf16[32,256]{1,0:T(8,128)(2,1)} %bitcast.13, bf16[144,16]{1,0:T(8,128)(2,1)} %bitcast.9, bf16[144,16]{1,0:T(8,128)(2,1)} %bitcast.10, bf16[144,16]{1,0:T(8,128)(2,1)} %bitcast.11), custom_call_target="tpu_custom_call" | custom-call | tf_op jit(solution)/shard_map/pallas_call | solution.py:315
  12.8 0.6 %copy.10 = bf16[4,1,32,128]{3,2,1,0:T(8,128)(2,1)} copy(bf16[4,1,32,128]{3,2,1,0:T(8,128)(2,1)S(1)} %bitcast.8) | data formatting | bytes 65536

commit v6 on v3

--- a/solution.py
+++ b/solution.py
@@ -58,6 +58,8 @@
     w1,
     w2,
     w3,
+    diagonal,
+    row_masks,
     local_sem,
     send_sem,
     recv_sem,
@@ -101,6 +103,21 @@
     ]
     for copy in own:
         copy.start()
+    zero_block = jnp.zeros((span, width), BF16)
+    vol[0] = zero_block
+    vol[breadth + 1] = zero_block
+    sec[1] = zero_block
+    sec[breadth] = zero_block
+    expand = (remainder(iota((groups, width), 1), groups) == iota((groups, width), 0)).astype(BF16)
+    lane_group = quotient(iota((groups, width), 1), groups)
+    lane_row = remainder(lane_group, window_rows)
+    nothing = jnp.zeros((groups, width), BF16)
+
+    one = jnp.ones((groups, width), BF16)
+    for j in range(width // groups):
+        diagonal[pl.ds(j * groups, groups), :] = jnp.where(lane_group == j, one, nothing)
+    for h in range(-1, window_rows + 1):
+        row_masks[h + 1] = jnp.where(lane_row == h, one, nothing)
     pl.semaphore_wait(barrier, src_count - 1 + (1 if tgt_count > 1 else 0))
 
     edge = pl.ds(pl.multiple_of((1 - half) * (rows - HALO), HALO), HALO)
@@ -156,19 +173,9 @@
     pl.when(has_right)(to_right.start)
     pl.when(has_left)(to_left.start)
 
-    zero_block = jnp.zeros((span, width), BF16)
-    vol[0] = zero_block
-    vol[breadth + 1] = zero_block
-    sec[1] = zero_block
-    sec[breadth] = zero_block
     for copy in own[2:5]:
         copy.wait()
-    expand = (remainder(iota((groups, width), 1), groups) == iota((groups, width), 0)).astype(BF16)
     spread = [dot(taps[i], expand).astype(BF16) for i in range(3)]
-    lane_group = quotient(iota((groups, width), 1), groups)
-    lane_row = remainder(lane_group, window_rows)
-    nothing = jnp.zeros((groups, width), BF16)
-
     def tap(i, a, b):
         start = (a * 3 + b) * groups
         return spread[i][start : start + groups]
@@ -176,8 +183,8 @@
     for a in range(3):
         for b in range(3):
             for j in range(width // groups):
-                w1[a, pl.ds(b * width + j * groups, groups), :] = jnp.where(
-                    lane_group == j, tap(0, a, b), nothing
+                w1[a, pl.ds(b * width + j * groups, groups), :] = (
+                    tap(0, a, b) * diagonal[pl.ds(j * groups, groups), :]
                 )
     for j in range(width // groups):
         k, h = divmod(j, window_rows)
@@ -185,10 +192,8 @@
         three = [nothing[:, :LANES]] * 3
         if k < 3:
             for a in range(3):
-                two = jnp.where(lane_row == h - a + 1, tap(1, a, k), two)
-                three[a] = jnp.where(
-                    (lane_row == h)[:, :LANES], tap(2, a, k)[:, :LANES], three[a]
-                )
+                two = two + tap(1, a, k) * row_masks[h - a + 2]
+                three[a] = tap(2, a, k)[:, :LANES] * row_masks[h + 1][:, :LANES]
         w2[pl.ds(j * groups, groups), :] = two
         for a in range(3):
             w3[pl.ds(j * groups, groups), pl.ds(a * LANES, LANES)] = three[a]
@@ -374,6 +379,8 @@
             pltpu.VMEM((3, 3 * width, width), BF16),
             pltpu.VMEM((width, width), BF16),
             pltpu.VMEM((width, 3 * LANES), BF16),
+            pltpu.VMEM((width, width), BF16),
+            pltpu.VMEM((window_rows + 2, groups, width), BF16),
             dma((7,)),
             dma((src_count,)),
             dma((src_count,)),

time: 12.7 us -> 12.7 us (level)
  no operation moved by 1% of the time
where the time goes in v6:
time: 12.7 us; the launch traced here: 12.5 us
  Pallas kernels  11.9 us (94%)
  local copies, waits for them, and re-layouts  0.62 us (5%)
    pallas_call x1, Pallas kernels, local(): pl.pallas_call(functools.partial(kernel, src_count, tgt_count, breadth, w...  11.9 us
    unnamed x1, local copies, waits for them, and re-layouts  0.62 us

profile of v6, /device:TPU:1, one launch (start us, length us, event | category | flops | bytes accessed | tf_op | source)
XLA Modules:
  0.0 12.5 jit_solution(341461121130656291)
XLA Ops:
  0.0 11.9 %shard_map.73 = bf16[4,32,128]{2,1,0:T(8,128)(2,1)S(1)} custom-call(s32[4]{0:T(128)} %rows_hbm.1, s32[8]{0:T(128)} %cols_hbm.1, bf16[32,256]{1,0:T(8,128)(2,1)} %bitcast.12, bf16[32,256]{1,0:T(8,128)(2,1)} %bitcast.13, bf16[144,16]{1,0:T(8,128)(2,1)} %bitcast.9, bf16[144,16]{1,0:T(8,128)(2,1)} %bitcast.10, bf16[144,16]{1,0:T(8,128)(2,1)} %bitcast.11), custom_call_target="tpu_custom_call" | custom-call | tf_op jit(solution)/shard_map/pallas_call | solution.py:362
  11.9 0.6 %copy.10 = bf16[4,1,32,128]{3,2,1,0:T(8,128)(2,1)} copy(bf16[4,1,32,128]{3,2,1,0:T(8,128)(2,1)S(1)} %bitcast.8) | data formatting | bytes 65536

commit v7 on v6

--- a/solution.py
+++ b/solution.py
@@ -47,7 +47,6 @@
     rows_ref,
     cols_ref,
     buf,
-    src_map,
     sbuf,
     taps,
     rim,
@@ -94,7 +93,7 @@
 
     own = [
         pltpu.make_async_copy(tgt_hbm, buf.at[me], local_sem.at[0]),
-        pltpu.make_async_copy(src_hbm, src_map, local_sem.at[1]),
+        pltpu.make_async_copy(src_hbm, sbuf.at[1], local_sem.at[1]),
         pltpu.make_async_copy(k1_hbm, taps.at[0], local_sem.at[2]),
         pltpu.make_async_copy(ks_hbm, taps.at[1], local_sem.at[3]),
         pltpu.make_async_copy(k2_hbm, taps.at[2], local_sem.at[4]),
@@ -124,11 +123,11 @@
     arrived = pl.ds(pl.multiple_of((1 - half) * rows, HALO), HALO)
 
     to_right = pltpu.make_async_remote_copy(
-        src_ref=sbuf.at[1], dst_ref=sbuf.at[0], send_sem=src_send.at[0], recv_sem=src_recv.at[0],
+        src_ref=src_hbm, dst_ref=sbuf.at[0], send_sem=src_send.at[0], recv_sem=src_recv.at[0],
         device_id={"src": lax.rem(me + 1, src_count)}, device_id_type=MESH,
     )
     to_left = pltpu.make_async_remote_copy(
-        src_ref=sbuf.at[1], dst_ref=sbuf.at[2], send_sem=src_send.at[1], recv_sem=src_recv.at[1],
+        src_ref=src_hbm, dst_ref=sbuf.at[2], send_sem=src_send.at[1], recv_sem=src_recv.at[1],
         device_id={"src": lax.rem(me + src_count - 1, src_count)}, device_id_type=MESH,
     )
     sends = []
@@ -140,6 +139,9 @@
             )
         )
     order = sorted(range(1, src_count), key=lambda d: -min(d, src_count - d))
+    has_left, has_right = me > 0, me < src_count - 1
+    pl.when(has_right)(to_right.start)
+    pl.when(has_left)(to_left.start)
     for d in order:
         sends[d - 1].start()
 
@@ -158,20 +160,6 @@
         offset = pl.multiple_of((1 - half) * (rows - HALO), HALO)
         forwards.append(forward(0, lambda column: tgt_hbm.at[pl.ds(offset, HALO)]))
         forwards[0].start()
-
-    has_left, has_right = me > 0, me < src_count - 1
-    own[1].wait()
-    own[5].wait()
-    own[6].wait()
-    picked = sbuf.shape[1]
-    row_of = iota((picked, map_rows), 0)
-    wanted = jnp.full((picked, map_rows), -1, jnp.int32)
-    for h in range(window_rows):
-        wanted = jnp.where(row_of == h, rows_ref[h], wanted)
-    choice = (iota((picked, map_rows), 1) == wanted).astype(BF16)
-    sbuf[1] = dot(choice, src_map[...]).astype(BF16)
-    pl.when(has_right)(to_right.start)
-    pl.when(has_left)(to_left.start)
 
     for copy in own[2:5]:
         copy.wait()
@@ -210,9 +198,14 @@
 
     pl.when(has_left)(to_right.wait_recv)
     pl.when(has_right)(to_left.wait_recv)
-    select = (
-        quotient(iota((column_lanes, picked), 0), groups) == iota((column_lanes, picked), 1)
-    ).astype(BF16)
+    own[1].wait()
+    own[5].wait()
+    own[6].wait()
+    row_of = quotient(iota((column_lanes, map_rows), 0), groups)
+    wanted = jnp.zeros((column_lanes, map_rows), jnp.int32)
+    for h in range(window_rows):
+        wanted = jnp.where(row_of == h, rows_ref[h], wanted)
+    select = (iota((column_lanes, map_rows), 1) == wanted).astype(BF16)
     same_group = (
         quotient(iota((column_lanes, features), 1), channels)
         == remainder(iota((column_lanes, features), 0), groups)
@@ -368,8 +361,7 @@
             pltpu.SMEM((window_rows,), jnp.int32),
             pltpu.SMEM((breadth,), jnp.int32),
             pltpu.VMEM((breadth, rows, features), BF16),
-            pltpu.VMEM((map_rows, features), BF16),
-            pltpu.VMEM((3, -(-window_rows // 16) * 16, features), BF16),
+            pltpu.VMEM((3, map_rows, features), BF16),
             pltpu.VMEM((3, taps, groups), BF16),
             pltpu.VMEM((breadth, HALO, features), BF16),
             pltpu.VMEM((breadth + 2, span, width), BF16),

time: 12.7 us -> 12.8 us (level)
  no operation moved by 1% of the time
where the time goes in v7:
time: 12.8 us; the launch traced here: 12.6 us
  Pallas kernels  12 us (94%)
  local copies, waits for them, and re-layouts  0.62 us (5%)
    pallas_call x1, Pallas kernels, local(): pl.pallas_call(functools.partial(kernel, src_count, tgt_count, breadth, w...  12 us
    unnamed x1, local copies, waits for them, and re-layouts  0.62 us

profile of v7, /device:TPU:1, one launch (start us, length us, event | category | flops | bytes accessed | tf_op | source)
XLA Modules:
  0.0 12.6 jit_solution(12267452834718743566)
XLA Ops:
  0.0 12.0 %shard_map.73 = bf16[4,32,128]{2,1,0:T(8,128)(2,1)S(1)} custom-call(s32[4]{0:T(128)} %rows_hbm.1, s32[8]{0:T(128)} %cols_hbm.1, bf16[32,256]{1,0:T(8,128)(2,1)} %bitcast.12, bf16[32,256]{1,0:T(8,128)(2,1)} %bitcast.13, bf16[144,16]{1,0:T(8,128)(2,1)} %bitcast.9, bf16[144,16]{1,0:T(8,128)(2,1)} %bitcast.10, bf16[144,16]{1,0:T(8,128)(2,1)} %bitcast.11), custom_call_target="tpu_custom_call" | custom-call | tf_op jit(solution)/shard_map/pallas_call | solution.py:355
  12.0 0.6 %copy.10 = bf16[4,1,32,128]{3,2,1,0:T(8,128)(2,1)} copy(bf16[4,1,32,128]{3,2,1,0:T(8,128)(2,1)S(1)} %bitcast.8) | data formatting | bytes 65536
